TPU v7x, 256 devices: a whole 4x4x8 slice. The times are simulated.
256 devices in a mesh: fsdp: 16 (over x, y), rep: 16 (over z, core).
Axes of the slice: x: 4, y: 4, z: 8, core: 2. Of those that a mesh axis runs over, the one named last changes fastest.
Arguments:
- momentum: float32 [28672, 8192], P('fsdp', 'rep'), may hold values from -6 to 6
- gradient: bfloat16 [28672, 8192], P('fsdp', 'rep'), may hold values from -6 to 6
- right_factor: float32 [8192, 256], P('rep'), may hold values from -6 to 6
Outputs:
- new_momentum: float32 [28672, 8192], P('fsdp', 'rep')
- new_factor: float32 [8192, 256], P('rep')
- update: bfloat16 [28672, 8192], P('fsdp', 'rep')
All inputs are finite; a program needn't handle non-finite values.
Results may differ from a plain program's by a relative error of at most 0.0014.
Values sent between devices are 32-bit elements; how exact they have to be, the bound alone decides.
A program may use at most 64 MiB of HBM per device.

v0:
```python
import functools
import math

import jax
import jax.numpy as jnp
from jax import lax
from jax.experimental import pallas as pl
from jax.experimental.pallas import tpu as pltpu
from jax.sharding import PartitionSpec as P

D = 8192
FF = 28672
R = 256

keep_share = 0.05
step_size = 0.5
norm_eps = 1e-06

F32 = jnp.float32
BF16 = jnp.bfloat16
MESH = pl.DeviceIdType.MESH
HIGHEST = lax.Precision.HIGHEST

ROWS = 1792
COLS = 512
NZ = 8
NF = 16
NR = 16
PAIR = ROWS // NZ
OWN = PAIR // 2
SUB = OWN // 2
NB = 32
TILE = 128


def split(x):
    hi = x.astype(BF16)
    return hi, (x - hi.astype(F32)).astype(BF16)


def dot(a, b, dims=((1,), (0,)), precision=None):
    return lax.dot_general(a, b, (dims, ((), ())), precision=precision, preferred_element_type=F32)


def dot3(a, b, dims=((1,), (0,))):
    return dot(a[0], b[0], dims) + (dot(a[1], b[0], dims) + dot(a[0], b[1], dims))


def factor_panel(rows, base):
    lane = lax.broadcasted_iota(jnp.int32, (8, 128), 1)
    sub = lax.broadcasted_iota(jnp.int32, (8, 128), 0)
    n = len(rows)
    for j in range(n):
        l0 = base + 8 * j
        half, at = l0 // 128, l0 % 128
        cols = [
            [jnp.broadcast_to(rows[i][half][:, at + c : at + c + 1], (8, 128)) for c in range(8)]
            for i in range(j, n)
        ]
        s = [
            [jnp.broadcast_to(cols[0][c][r : r + 1, :], (8, 128)) if r >= c else None for c in range(8)]
            for r in range(8)
        ]
        inv, low, solved = [None] * 8, [[None] * 8 for _ in range(8)], []
        own = (lane >= at) & (lane < at + 8)
        v = list(rows[j])
        v[half] = jnp.where(own, jnp.where(lane - at == sub, 1.0, 0.0), v[half])
        for p in range(8):
            inv[p] = lax.rsqrt(s[p][p])
            for r in range(p + 1, 8):
                low[r][p] = s[r][p] * inv[p]
            for r in range(p + 1, 8):
                for c in range(p + 1, r + 1):
                    s[r][c] = s[r][c] - low[r][p] * low[c][p]
            x = [jnp.broadcast_to(v[h][p : p + 1, :], (8, 128)) for h in range(2)]
            for q in range(p):
                x = [x[h] - low[p][q] * solved[q][h] for h in range(2)]
            solved.append([x[h] * inv[p] for h in range(2)])
        for i in range(j + 1, n):
            w, coef = list(rows[i]), []
            w[half] = jnp.where(own, 0.0, w[half])
            for p in range(8):
                t = cols[i - j][p]
                for q in range(p):
                    t = t - coef[q] * low[p][q]
                coef.append(t * inv[p])
            for p in range(8):
                w = [w[h] - coef[p] * solved[p][h] for h in range(2)]
            rows[i] = w
        out = []
        for h in range(2):
            a = solved[0][h]
            for p in range(1, 8):
                a = jnp.where(sub == p, solved[p][h], a)
            out.append(a)
        rows[j] = out
    return rows


def chol_step(M, k):
    r0, end = NB * k, NB * (k + 1)
    rows = [
        [M[r0 + 8 * j : r0 + 8 * j + 8, 128 * h : 128 * h + 128] for h in range(2)] for j in range(NB // 8)
    ]
    rows = factor_panel(rows, r0)
    for j in range(NB // 8):
        for h in range(2):
            M[r0 + 8 * j : r0 + 8 * j + 8, 128 * h : 128 * h + 128] = rows[j][h]
    if end == R:
        return
    panel = M[r0:end, :]
    row = lax.broadcasted_iota(jnp.int32, (NB, R), 0) + r0
    col = lax.broadcasted_iota(jnp.int32, (NB, R), 1)
    right = jnp.where((col < end) & (col > row), 0.0, panel)
    lo = (end // 128) * 128
    left = jnp.swapaxes(panel[:, lo:], 0, 1)[end - lo :, :]
    old = M[end:, :]
    at = lax.broadcasted_iota(jnp.int32, old.shape, 1)
    old = jnp.where((at >= r0) & (at < end), 0.0, old)
    M[end : end + NB, :] = old[:NB] - dot(left[:NB], right, precision=HIGHEST)
    if end + NB < R:
        M[end + NB :, :] = old[NB:] - dot(left[NB:], right, precision=HIGHEST)


def gather_kernel(
    mom, grad, q_hbm, nm_out, u_out, wt_out, inv_out,
    momb, gradb, qb, chi, clo, part, sib, rsr, pfull, gp, g1, g2, gs, gf, M, yp, yr, yf, y8, g16, cs, csr,
    ld_sem, q_sem, sib_s, sib_r, rs_s, rs_r, ag_s, ag_r, sb_s, sb_r, g_s, g_r, y_s, y_r, n_s, n_r,
):
    f, r = lax.axis_index("fsdp"), lax.axis_index("rep")
    z, c = r // 2, r % 2
    sibling = (f, z * 2 + 1 - c)
    ring = ((f, ((z + 1) % NZ) * 2 + c), (f, ((z + NZ - 1) % NZ) * 2 + c))
    mine = pl.multiple_of(c * OWN, 8)
    other = pl.multiple_of((1 - c) * OWN, 8)
    HALVES, WAYS = range(2), range(2)

    def lanes(h):
        return pl.ds(128 * h, 128)

    def sub_at(s):
        return pl.ds(pl.multiple_of(c * OWN + s * SUB, 8), SUB)

    def remote(src, dst, ss, rs, to):
        return pltpu.make_async_remote_copy(src, dst, ss, rs, device_id=to, device_id_type=MESH)

    q_load = pltpu.make_async_copy(q_hbm, qb, q_sem)
    q_load.start()
    loads = {}
    for o in (4, 3, 5, 2, 6, 1, 7, 0):
        zd = (z + o) % NZ
        at = pl.ds(pl.multiple_of(zd * PAIR, PAIR), PAIR)
        loads[o] = (
            pltpu.make_async_copy(mom.at[at], momb.at[o], ld_sem.at[0, o]),
            pltpu.make_async_copy(grad.at[at], gradb.at[o], ld_sem.at[1, o]),
        )
        for copy in loads[o]:
            copy.start()

    barrier = pltpu.get_barrier_semaphore()

    @pl.loop(1, 16)
    def _(k):
        pl.semaphore_signal(barrier, 1, device_id=(f, (r + k) % NR), device_id_type=MESH)
        pl.semaphore_signal(barrier, 1, device_id=((f + k) % NF, r), device_id_type=MESH)

    q_load.wait()
    q = split(qb[...])
    sends = []

    def go(copy):
        copy.start()
        sends.append(copy)
        return copy

    sib_copy = {}

    def compute(o):
        for copy in loads[o]:
            copy.wait()
        zd = (z + o) % NZ
        combined = momb[o] + gradb[o].astype(F32)
        momb[o] = combined
        both = split(combined)
        chi[zd] = both[0]
        clo[zd] = both[1]
        part[o] = dot3(both, q)

    def to_sibling(o):
        sib_copy[o] = go(
            remote(part.at[o, pl.ds(other, OWN)], sib.at[o], sib_s.at[o], sib_r.at[o], sibling)
        )

    def add_sibling(o):
        sib_copy[o].wait_recv()
        part[o, pl.ds(mine, OWN)] = part[o, pl.ds(mine, OWN)] + sib[o]

    def offset(way, level):
        return level if way == 0 else (NZ - level) % NZ

    rs_copy = {}

    def rs_send(way, level, s, h):
        at = (way, level - 1, h, s)
        rs_copy[at] = go(
            remote(
                part.at[offset(way, level), sub_at(s), lanes(h)],
                rsr.at[at], rs_s.at[at], rs_r.at[at], ring[way],
            )
        )

    def rs_add(way, level, s, h):
        at = (way, level, h, s)
        rs_copy[at].wait_recv()
        o = offset(way, level)
        part[o, sub_at(s), lanes(h)] = part[o, sub_at(s), lanes(h)] + rsr[at]

    def rs_pass(level, late):
        for h in HALVES:
            for way in WAYS:
                s = way if late else 1 - way
                rs_add(way, level, s, h)
                rs_send(way, level, s, h)

    compute(4)
    compute(3)
    pl.semaphore_wait(barrier, 30)
    to_sibling(4)
    to_sibling(3)
    compute(5)
    to_sibling(5)
    add_sibling(4)
    for h in HALVES:
        for way in WAYS:
            rs_send(way, 4, way, h)
    add_sibling(3)
    for h in HALVES:
        rs_send(0, 3, 1, h)
    add_sibling(5)
    for h in HALVES:
        rs_send(1, 3, 0, h)
    compute(2)
    to_sibling(2)
    compute(6)
    to_sibling(6)
    compute(1)
    to_sibling(1)
    add_sibling(2)
    add_sibling(6)
    rs_pass(3, True)
    compute(7)
    to_sibling(7)
    rs_pass(2, False)
    compute(0)
    to_sibling(0)
    add_sibling(1)
    add_sibling(7)
    rs_pass(2, True)
    rs_pass(1, False)
    add_sibling(0)
    rs_pass(1, True)

    ag_copy, sb_copy = {}, {}

    def source(way, level):
        return (z + (NZ - level if way == 0 else level)) % NZ

    def ag_send(way, level, h, s):
        at = (way, level - 1, h, s)
        ref = pfull.at[h, source(way, level - 1), sub_at(s)]
        ag_copy[at] = go(remote(ref, ref, ag_s.at[at], ag_r.at[at], ring[way]))

    def sb_send(way, level, h):
        rows = sub_at(way) if level == 4 else pl.ds(mine, OWN)
        ref = pfull.at[h, source(way, level), rows]
        at = (way, level, h)
        sb_copy[at] = go(remote(ref, ref, sb_s.at[at], sb_r.at[at], sibling))

    for h in HALVES:
        for late in (False, True):
            for way in WAYS:
                rs_add(way, 0, way if late else 1 - way, h)
        pfull[h, z, pl.ds(mine, OWN), :] = part[0, pl.ds(mine, OWN), lanes(h)]
        for s in range(2):
            for way in WAYS:
                ag_send(way, 1, h, s)
        sb_send(0, 0, h)

    def to_all(src_of, dst, send, recv, along):
        me, n = {"rep": (r, NR), "fsdp": (f, NF), "z": (z, NZ)}[along]

        @pl.loop(1, n)
        def _(k):
            peer = (me + k) % n
            to = {"rep": (f, peer), "fsdp": (peer, r), "z": (f, peer * 2 + c)}[along]
            remote(src_of(peer), dst.at[me], send, recv, to).start()

    def span_wait(dst, sem):
        span = dst.at[pl.ds(0, dst.shape[0] - 1)]
        pltpu.make_async_copy(span, span, sem).wait()

    def total(ref):
        t = ref[0]
        for k in range(1, ref.shape[0]):
            t = t + ref[k]
        return t

    own_rows = part[0, pl.ds(mine, OWN), :]
    gp[...] = dot(own_rows, own_rows, ((0,), (0,)), HIGHEST).reshape(16, 16, R)
    to_all(lambda peer: gp.at[peer], g1, g_s.at[0], g_r.at[0], "fsdp")
    g1[pl.ds(f, 1)] = gp[pl.ds(f, 1)]

    def ag_pass(level):
        for h in HALVES:
            for s in range(2):
                for way in WAYS:
                    ag_copy[way, level - 1, h, s].wait_recv()
                    if level < 3 or s == way:
                        ag_send(way, level + 1, h, s)
            for way in WAYS:
                sb_send(way, level, h)

    def y_add(zs, h, first=False):
        p = split(jnp.swapaxes(pfull[h, zs], 0, 1))
        y = dot3(p, (chi[zs], clo[zs]))
        yp[h] = y if first else yp[h] + y

    def y_level(level, h):
        for way in WAYS:
            if (way, level, h) in sb_copy:
                sb_copy[way, level, h].wait_recv()
        for way in range(2 if 0 < level < 4 else 1):
            y_add(source(way, level), h, level == 0)

    def y_scatter(h):
        to_all(lambda peer: yp.at[h, pl.ds(pl.multiple_of(peer * 8, 8), 8)], yr.at[h], y_s.at[h], y_r.at[h], "fsdp")
        yr[h, pl.ds(f, 1)] = yp[h, pl.ds(pl.multiple_of(f * 8, 8), 8)].reshape(1, 8, COLS)

    def y_gather(h):
        span_wait(yr.at[h], y_r.at[h])
        y8[h] = total(yr.at[h])
        to_all(lambda peer: y8.at[h], yf.at[h], y_s.at[2 + h], y_r.at[2 + h], "fsdp")
        yf[h, pl.ds(f, 1)] = y8[pl.ds(h, 1)]

    ag_pass(1)
    for h in HALVES:
        y_level(0, h)
    ag_pass(2)
    span_wait(g1, g_r.at[0])
    g16[0] = total(g1)
    to_all(lambda peer: g16.at[0], g2, g_s.at[1], g_r.at[1], "z")
    g2[pl.ds(z, 1)] = g16[pl.ds(0, 1)]
    for h in HALVES:
        y_level(1, h)
    ag_pass(3)
    span_wait(g2, g_r.at[1])
    g16[1] = total(g2)
    g_copy = go(remote(g16.at[1], gs, g_s.at[3], g_r.at[3], sibling))
    for h in HALVES:
        y_level(2, h)
    g_copy.wait_recv()
    g16[2] = g16[1] + gs[...]
    to_all(lambda peer: g16.at[2], gf, g_s.at[2], g_r.at[2], "fsdp")
    gf[pl.ds(f, 1)] = g16[pl.ds(2, 1)]
    for h in HALVES:
        for way in WAYS:
            ag_copy[way, 3, h, way].wait_recv()
            sb_send(way, 4, h)
        y_level(3, h)
    for h in HALVES:
        y_level(4, h)
        y_scatter(h)
    span_wait(gf, g_r.at[2])
    M[...] = gf[...].reshape(R, R)
    for k in range(R // NB):
        if k == 4:
            y_gather(0)
            y_gather(1)
        chol_step(M, k)
    row = lax.broadcasted_iota(jnp.int32, (R, R), 0)
    col = lax.broadcasted_iota(jnp.int32, (R, R), 1)
    M[...] = jnp.where(col <= row, M[...], 0.0)
    for h in HALVES:
        span_wait(yf.at[h], y_r.at[2 + h])
    wt = dot3(split(M[...]), split(yf[...].reshape(R, COLS)))
    wt_out[...] = wt
    cs[...] = dot(jnp.ones((8, COLS), F32), wt * wt, ((1,), (1,)), HIGHEST)
    to_all(lambda peer: cs, csr, n_s, n_r, "rep")
    csr[pl.ds(r, 1)] = cs[...].reshape(1, 8, R)

    @pl.loop(0, NZ)
    def _(o):
        zs = (z + o) % NZ
        t = jnp.concatenate([pfull[0, zs], pfull[1, zs]], axis=1)
        u = dot3(split(t), split(M[...]), ((1,), (1,)))
        u_out[zs] = u
        nm_out[zs] = momb[o] - keep_share * dot(u.astype(BF16), wt_out[...].astype(BF16))

    span_wait(csr, n_r)
    inv_out[...] = 1.0 / jnp.sqrt(total(csr) / D + norm_eps)
    for copy in sends:
        copy.wait_send()
    for k, ref in enumerate((g1, g2, gf)):
        span_wait(ref, g_s.at[k])
    for h in HALVES:
        span_wait(yr.at[h], y_s.at[h])
        span_wait(yf.at[h], y_s.at[2 + h])
    span_wait(csr, n_s)


def gather(mom, grad, q):
    dma = pltpu.SemaphoreType.DMA
    vm = pltpu.VMEM
    scratch = [
        vm((NZ, PAIR, COLS), F32), vm((NZ, PAIR, COLS), BF16), vm((COLS, R), F32),
        vm((NZ, PAIR, COLS), BF16), vm((NZ, PAIR, COLS), BF16),
        vm((NZ, PAIR, R), F32), vm((NZ, OWN, R), F32), vm((2, 4, 2, 2, SUB, 128), F32), vm((2, NZ, PAIR, 128), F32),
        vm((16, 16, R), F32), vm((16, 16, R), F32), vm((NZ, 16, R), F32), vm((16, R), F32), vm((16, 16, R), F32),
        vm((R, R), F32),
        vm((2, 128, COLS), F32), vm((2, 16, 8, COLS), F32), vm((2, 16, 8, COLS), F32), vm((2, 8, COLS), F32),
        vm((3, 16, R), F32), vm((8, R), F32), vm((16, 8, R), F32),
        dma((2, NZ)), dma, dma((NZ,)), dma((NZ,)), dma((2, 4, 2, 2)), dma((2, 4, 2, 2)),
        dma((2, 4, 2, 2)), dma((2, 4, 2, 2)), dma((2, 5, 2)), dma((2, 5, 2)),
        dma((4,)), dma((4,)), dma((4,)), dma((4,)), dma, dma,
    ]
    whole, hbm = pl.BlockSpec(memory_space=pltpu.VMEM), pl.BlockSpec(memory_space=pl.ANY)
    return pl.pallas_call(
        gather_kernel,
        name="gather",
        out_shape=(
            pltpu.VMEM((NZ, PAIR, COLS), F32),
            pltpu.VMEM((NZ, PAIR, R), F32),
            pltpu.VMEM((R, COLS), F32),
            pltpu.VMEM((8, R), F32),
        ),
        in_specs=[hbm, hbm, hbm],
        out_specs=(whole, whole, whole, whole),
        scratch_shapes=scratch,
        compiler_params=pltpu.CompilerParams(
            collective_id=0, has_side_effects=True, vmem_limit_bytes=40 << 20
        ),
    )(*(pltpu.with_memory_space_constraint(x, pltpu.HBM) for x in (mom, grad, q)))


def result_kernel(
    nm, u_ref, wt_ref, inv_ref, new_mom, new_factor, update, ub, fb, wh, wl, m_sem, u_sem, f_sem
):
    def tile(i):
        return pl.ds(i * TILE, TILE)

    copies = []
    for i in range(ROWS // TILE):
        copies.append(pltpu.make_async_copy(nm.at[tile(i)], new_mom.at[tile(i)], m_sem.at[i]))
        copies[-1].start()
    inv = inv_ref[0:1, :]
    wh[...], wl[...] = split(wt_ref[...])
    for i in range(ROWS // TILE):
        scaled = split(u_ref[tile(i), :] * (inv * (-step_size * math.sqrt(FF / R))))
        ub[tile(i), :] = dot3(scaled, (wh[...], wl[...])).astype(BF16)
        copies.append(pltpu.make_async_copy(ub.at[tile(i)], update.at[tile(i)], u_sem.at[i]))
        copies[-1].start()
        if i == 0:
            fb[...] = jnp.swapaxes(wt_ref[...], 0, 1) * inv
            copies.append(pltpu.make_async_copy(fb, new_factor, f_sem))
            copies[-1].start()
    for copy in copies:
        copy.wait()


def results(nm, u, wt, inv):
    vmem, hbm = pl.BlockSpec(memory_space=pltpu.VMEM), pl.BlockSpec(memory_space=pl.ANY)
    dma = pltpu.SemaphoreType.DMA
    return pl.pallas_call(
        result_kernel,
        name="results",
        out_shape=(
            jax.ShapeDtypeStruct((ROWS, COLS), F32),
            jax.ShapeDtypeStruct((COLS, R), F32),
            jax.ShapeDtypeStruct((ROWS, COLS), BF16),
        ),
        in_specs=[vmem, vmem, vmem, vmem],
        out_specs=(hbm, hbm, hbm),
        scratch_shapes=[
            pltpu.VMEM((ROWS, COLS), BF16),
            pltpu.VMEM((COLS, R), F32),
            pltpu.VMEM((R, COLS), BF16),
            pltpu.VMEM((R, COLS), BF16),
            dma((ROWS // TILE,)),
            dma((ROWS // TILE,)),
            dma,
        ],
        compiler_params=pltpu.CompilerParams(vmem_limit_bytes=32 << 20),
    )(nm, u, wt, inv)


def local(momentum, gradient, right_factor):
    nm, u, wt, inv = gather(momentum, gradient, right_factor)
    return results(nm.reshape(ROWS, COLS), u.reshape(ROWS, R), wt, inv)


def solution(mesh):
    in_specs = (P("fsdp", "rep"), P("fsdp", "rep"), P("rep", None))
    out_specs = (P("fsdp", "rep"), P("rep", None), P("fsdp", "rep"))
    return jax.shard_map(local, mesh=mesh, in_specs=in_specs, out_specs=out_specs, check_vma=False)
```

profile of v0, /device:TPU:1, one launch (start us, length us, event | category | flops | bytes accessed | tf_op | source)
XLA Modules:
  0.0 74.2 jit_solution(8246469223763365983)
XLA Ops:
  0.6 69.7 %gather.1 = (f32[8,224,512]{2,1,0:T(8,128)S(1)}, f32[8,224,256]{2,1,0:T(8,128)S(1)}, f32[256,512]{1,0:T(8,128)S(1)}, f32[8,256]{1,0:T(8,128)S(1)}) custom-call(f32[1792,512]{1,0:T(8,128)} %mom.1, bf16[1792,512]{1,0:T(8,128)(2,1)} %grad.1, f32[512,256]{1,0:T(8,128)} %q_hbm.1), custom_call_target="tpu_custom_call" | custom-call | tf_op jit(solution)/shard_map/gather/pallas_call | solution.py:427
  70.3 3.7 %results.1 = (f32[1792,512]{1,0:T(8,128)}, f32[512,256]{1,0:T(8,128)}, bf16[1792,512]{1,0:T(8,128)(2,1)}) custom-call(f32[1792,512]{1,0:T(8,128)S(1)} %bitcast.2, f32[1792,256]{1,0:T(8,128)S(1)} %bitcast.3, f32[256,512]{1,0:T(8,128)S(1)} %get-tuple-element.9.wt_ref, f32[8,256]{1,0:T(8,128)S(1)} %get-tuple-element.10.inv_ref), custom_call_target="tpu_custom_call" | custom-call | tf_op jit(solution)/shard_map/results/pallas_call | solution.py:473
where the time goes:
time: 74.2 us
  Pallas kernels  73.4 us (99%)
  between operations  0.8 us (1%)
    pallas_call x1, Pallas kernels, gather(): pl.pallas_call(gather_kernel, name='gather', out_shape=(pltpu.VMEM((NZ, P...  69.7 us
    pallas_call x1, Pallas kernels, results(): pl.pallas_call(result_kernel, name='results', out_shape=(jax.ShapeDtypeSt...  3.69 us

commit v1 on v0

--- a/solution.py
+++ b/solution.py
@@ -123,8 +123,8 @@
 
 
 def gather_kernel(
-    mom, grad, q_hbm, nm_out, u_out, wt_out, inv_out,
-    momb, gradb, qb, chi, clo, part, sib, rsr, pfull, gp, g1, g2, gs, gf, M, yp, yr, yf, y8, g16, cs, csr,
+    mom, grad, q_hbm, nm_out, uh_out, ul_out, wt_out, inv_out,
+    momb, gradb, qb, chi, clo, part, sib, rsr, pfull, gp, g1, g2, gs, gf, gh, M, yp, yr, yf, y8, g16, cs, csr, lth, ltl, wh,
     ld_sem, q_sem, sib_s, sib_r, rs_s, rs_r, ag_s, ag_r, sb_s, sb_r, g_s, g_r, y_s, y_r, n_s, n_r,
 ):
     f, r = lax.axis_index("fsdp"), lax.axis_index("rep")
@@ -134,12 +134,22 @@
     mine = pl.multiple_of(c * OWN, 8)
     other = pl.multiple_of((1 - c) * OWN, 8)
     HALVES, WAYS = range(2), range(2)
+    x, y = f // 4, f % 4
+    steps = sorted(((dx, dy) for dx in range(4) for dy in range(4)), key=lambda d: -(d[0] % 3 + d[0] // 3 + d[1] % 3 + d[1] // 3))
+    peers = {
+        "fsdp": [((x + dx) % 4) * 4 + (y + dy) % 4 for dx, dy in steps if (dx, dy) != (0, 0)],
+        "z": [(z + dz) % NZ for dz in (4, 3, 5, 2, 6, 1, 7)],
+    }
+    peers["rep"] = [zp * 2 + cp for zp in peers["z"] for cp in (1 - c, c)] + [z * 2 + 1 - c]
 
     def lanes(h):
         return pl.ds(128 * h, 128)
 
     def sub_at(s):
         return pl.ds(pl.multiple_of(c * OWN + s * SUB, 8), SUB)
+
+    def slot(o):
+        return (o + 3) % NZ
 
     def remote(src, dst, ss, rs, to):
         return pltpu.make_async_remote_copy(src, dst, ss, rs, device_id=to, device_id_type=MESH)
@@ -151,8 +161,8 @@
         zd = (z + o) % NZ
         at = pl.ds(pl.multiple_of(zd * PAIR, PAIR), PAIR)
         loads[o] = (
-            pltpu.make_async_copy(mom.at[at], momb.at[o], ld_sem.at[0, o]),
-            pltpu.make_async_copy(grad.at[at], gradb.at[o], ld_sem.at[1, o]),
+            pltpu.make_async_copy(mom.at[at], momb.at[slot(o)], ld_sem.at[0, o]),
+            pltpu.make_async_copy(grad.at[at], gradb.at[slot(o)], ld_sem.at[1, o]),
         )
         for copy in loads[o]:
             copy.start()
@@ -178,12 +188,11 @@
     def compute(o):
         for copy in loads[o]:
             copy.wait()
-        zd = (z + o) % NZ
-        combined = momb[o] + gradb[o].astype(F32)
-        momb[o] = combined
+        combined = momb[slot(o)] + gradb[slot(o)].astype(F32)
+        momb[slot(o)] = combined
         both = split(combined)
-        chi[zd] = both[0]
-        clo[zd] = both[1]
+        chi[slot(o)] = both[0]
+        clo[slot(o)] = both[1]
         part[o] = dot3(both, q)
 
     def to_sibling(o):
@@ -263,35 +272,30 @@
     ag_copy, sb_copy = {}, {}
 
     def source(way, level):
-        return (z + (NZ - level if way == 0 else level)) % NZ
+        return slot(-level if way == 0 else level)
 
     def ag_send(way, level, h, s):
         at = (way, level - 1, h, s)
         ref = pfull.at[h, source(way, level - 1), sub_at(s)]
-        ag_copy[at] = go(remote(ref, ref, ag_s.at[at], ag_r.at[at], ring[way]))
-
-    def sb_send(way, level, h):
-        rows = sub_at(way) if level == 4 else pl.ds(mine, OWN)
-        ref = pfull.at[h, source(way, level), rows]
-        at = (way, level, h)
-        sb_copy[at] = go(remote(ref, ref, sb_s.at[at], sb_r.at[at], sibling))
+        dst = pfull.at[h, source(way, level), sub_at(s)]
+        ag_copy[at] = go(remote(ref, dst, ag_s.at[at], ag_r.at[at], ring[way]))
+
+    def sb_send(i, first, end, h=None):
+        ref = pfull.at[slice(None) if h is None else pl.ds(h, 1), pl.ds(first, end - first), pl.ds(mine, OWN)]
+        sb_copy[i] = go(remote(ref, ref, sb_s.at[i], sb_r.at[i], sibling))
 
     for h in HALVES:
         for late in (False, True):
             for way in WAYS:
                 rs_add(way, 0, way if late else 1 - way, h)
-        pfull[h, z, pl.ds(mine, OWN), :] = part[0, pl.ds(mine, OWN), lanes(h)]
+        pfull[h, slot(0), pl.ds(mine, OWN), :] = part[0, pl.ds(mine, OWN), lanes(h)]
         for s in range(2):
             for way in WAYS:
                 ag_send(way, 1, h, s)
-        sb_send(0, 0, h)
 
     def to_all(src_of, dst, send, recv, along):
-        me, n = {"rep": (r, NR), "fsdp": (f, NF), "z": (z, NZ)}[along]
-
-        @pl.loop(1, n)
-        def _(k):
-            peer = (me + k) % n
+        me = {"rep": r, "fsdp": f, "z": z}[along]
+        for peer in peers[along]:
             to = {"rep": (f, peer), "fsdp": (peer, r), "z": (f, peer * 2 + c)}[along]
             remote(src_of(peer), dst.at[me], send, recv, to).start()
 
@@ -310,27 +314,17 @@
     to_all(lambda peer: gp.at[peer], g1, g_s.at[0], g_r.at[0], "fsdp")
     g1[pl.ds(f, 1)] = gp[pl.ds(f, 1)]
 
-    def ag_pass(level):
-        for h in HALVES:
-            for s in range(2):
-                for way in WAYS:
-                    ag_copy[way, level - 1, h, s].wait_recv()
-                    if level < 3 or s == way:
-                        ag_send(way, level + 1, h, s)
+    def ag_pass(level, h):
+        for s in range(2):
             for way in WAYS:
-                sb_send(way, level, h)
-
-    def y_add(zs, h, first=False):
-        p = split(jnp.swapaxes(pfull[h, zs], 0, 1))
-        y = dot3(p, (chi[zs], clo[zs]))
-        yp[h] = y if first else yp[h] + y
-
-    def y_level(level, h):
-        for way in WAYS:
-            if (way, level, h) in sb_copy:
-                sb_copy[way, level, h].wait_recv()
-        for way in range(2 if 0 < level < 4 else 1):
-            y_add(source(way, level), h, level == 0)
+                ag_copy[way, level - 1, h, s].wait_recv()
+                if level < 3 or s == way:
+                    ag_send(way, level + 1, h, s)
+
+    def y_add(first, end, h):
+        deep = (end - first) * PAIR
+        p = split(jnp.swapaxes(pfull[h, first:end].reshape(deep, 128), 0, 1))
+        return dot3(p, (chi[first:end].reshape(deep, COLS), clo[first:end].reshape(deep, COLS)))
 
     def y_scatter(h):
         to_all(lambda peer: yp.at[h, pl.ds(pl.multiple_of(peer * 8, 8), 8)], yr.at[h], y_s.at[h], y_r.at[h], "fsdp")
@@ -342,40 +336,51 @@
         to_all(lambda peer: y8.at[h], yf.at[h], y_s.at[2 + h], y_r.at[2 + h], "fsdp")
         yf[h, pl.ds(f, 1)] = y8[pl.ds(h, 1)]
 
-    ag_pass(1)
-    for h in HALVES:
-        y_level(0, h)
-    ag_pass(2)
+    ag_pass(1, 0)
+    ag_pass(1, 1)
+    ag_pass(2, 0)
     span_wait(g1, g_r.at[0])
-    g16[0] = total(g1)
-    to_all(lambda peer: g16.at[0], g2, g_s.at[1], g_r.at[1], "z")
-    g2[pl.ds(z, 1)] = g16[pl.ds(0, 1)]
-    for h in HALVES:
-        y_level(1, h)
-    ag_pass(3)
-    span_wait(g2, g_r.at[1])
-    g16[1] = total(g2)
-    g_copy = go(remote(g16.at[1], gs, g_s.at[3], g_r.at[3], sibling))
-    for h in HALVES:
-        y_level(2, h)
+    g16[...] = total(g1)
+    my_half = pl.ds(pl.multiple_of(c * 8, 8), 8)
+    g_copy = go(
+        remote(g16.at[pl.ds(pl.multiple_of((1 - c) * 8, 8), 8)], gs, g_s.at[3], g_r.at[3], sibling)
+    )
+    ag_pass(2, 1)
+    sb_send(0, 1, 6)
     g_copy.wait_recv()
-    g16[2] = g16[1] + gs[...]
-    to_all(lambda peer: g16.at[2], gf, g_s.at[2], g_r.at[2], "fsdp")
-    gf[pl.ds(f, 1)] = g16[pl.ds(2, 1)]
+    gh[0] = g16[my_half, :] + gs[...]
+    to_all(lambda peer: gh.at[0], g2, g_s.at[1], g_r.at[1], "z")
+    g2[pl.ds(z, 1)] = gh[pl.ds(0, 1)]
+    ag_pass(3, 0)
+    ag_pass(3, 1)
+    sb_send(1, 0, 1)
+    sb_send(2, 6, 7)
+    sb_copy[0].wait_recv()
+    for h in HALVES:
+        yp[h] = y_add(1, 6, h)
     for h in HALVES:
         for way in WAYS:
             ag_copy[way, 3, h, way].wait_recv()
-            sb_send(way, 4, h)
-        y_level(3, h)
-    for h in HALVES:
-        y_level(4, h)
+        sb_send(3 + h, 7, 8, h)
+    span_wait(g2, g_r.at[1])
+    gh[1] = total(g2)
+    to_all(lambda peer: gh.at[1], gf.at[c], g_s.at[2], g_r.at[2], "fsdp")
+    gf[c, pl.ds(f, 1)] = gh[pl.ds(1, 1)]
+    sb_copy[1].wait_recv()
+    sb_copy[2].wait_recv()
+    for h in HALVES:
+        yp[h] = yp[h] + (y_add(0, 1, h) + y_add(6, 7, h))
+    for h in HALVES:
+        sb_copy[3 + h].wait_recv()
+        yp[h] = yp[h] + y_add(7, 8, h)
         y_scatter(h)
-    span_wait(gf, g_r.at[2])
-    M[...] = gf[...].reshape(R, R)
+    span_wait(gf.at[0], g_r.at[2])
+    g_copy = go(remote(gf.at[c], gf.at[c], g_s.at[4], g_r.at[4], sibling))
+    for h in HALVES:
+        y_gather(h)
+    g_copy.wait_recv()
+    M[...] = jnp.stack([gf[0], gf[1]], axis=1).reshape(R, R)
     for k in range(R // NB):
-        if k == 4:
-            y_gather(0)
-            y_gather(1)
         chol_step(M, k)
     row = lax.broadcasted_iota(jnp.int32, (R, R), 0)
     col = lax.broadcasted_iota(jnp.int32, (R, R), 1)
@@ -384,23 +389,30 @@
         span_wait(yf.at[h], y_r.at[2 + h])
     wt = dot3(split(M[...]), split(yf[...].reshape(R, COLS)))
     wt_out[...] = wt
-    cs[...] = dot(jnp.ones((8, COLS), F32), wt * wt, ((1,), (1,)), HIGHEST)
+    square = wt * wt
+    square = (square[:, :128] + square[:, 128:256]) + (square[:, 256:384] + square[:, 384:])
+    cs[...] = jnp.broadcast_to(jnp.sum(jnp.swapaxes(square, 0, 1), axis=0, keepdims=True), (8, R))
     to_all(lambda peer: cs, csr, n_s, n_r, "rep")
     csr[pl.ds(r, 1)] = cs[...].reshape(1, 8, R)
 
+    lth[...], ltl[...] = split(jnp.swapaxes(M[...], 0, 1))
+    wh[...] = wt.astype(BF16)
+
     @pl.loop(0, NZ)
-    def _(o):
-        zs = (z + o) % NZ
-        t = jnp.concatenate([pfull[0, zs], pfull[1, zs]], axis=1)
-        u = dot3(split(t), split(M[...]), ((1,), (1,)))
-        u_out[zs] = u
-        nm_out[zs] = momb[o] - keep_share * dot(u.astype(BF16), wt_out[...].astype(BF16))
+    def _(k):
+        zs = (z + k + NZ - 3) % NZ
+        t = jnp.concatenate([pfull[0, k], pfull[1, k]], axis=1)
+        u = dot3(split(t), (lth[...], ltl[...]))
+        u = split(u)
+        uh_out[zs] = u[0]
+        ul_out[zs] = u[1]
+        nm_out[zs] = momb[k] - keep_share * dot(u[0], wh[...])
 
     span_wait(csr, n_r)
     inv_out[...] = 1.0 / jnp.sqrt(total(csr) / D + norm_eps)
     for copy in sends:
         copy.wait_send()
-    for k, ref in enumerate((g1, g2, gf)):
+    for k, ref in enumerate((g1, g2, gf.at[0])):
         span_wait(ref, g_s.at[k])
     for h in HALVES:
         span_wait(yr.at[h], y_s.at[h])
@@ -415,13 +427,15 @@
         vm((NZ, PAIR, COLS), F32), vm((NZ, PAIR, COLS), BF16), vm((COLS, R), F32),
         vm((NZ, PAIR, COLS), BF16), vm((NZ, PAIR, COLS), BF16),
         vm((NZ, PAIR, R), F32), vm((NZ, OWN, R), F32), vm((2, 4, 2, 2, SUB, 128), F32), vm((2, NZ, PAIR, 128), F32),
-        vm((16, 16, R), F32), vm((16, 16, R), F32), vm((NZ, 16, R), F32), vm((16, R), F32), vm((16, 16, R), F32),
+        vm((16, 16, R), F32), vm((16, 16, R), F32), vm((NZ, 8, R), F32), vm((8, R), F32), vm((2, 16, 8, R), F32),
+        vm((2, 8, R), F32),
         vm((R, R), F32),
         vm((2, 128, COLS), F32), vm((2, 16, 8, COLS), F32), vm((2, 16, 8, COLS), F32), vm((2, 8, COLS), F32),
-        vm((3, 16, R), F32), vm((8, R), F32), vm((16, 8, R), F32),
+        vm((16, R), F32), vm((8, R), F32), vm((16, 8, R), F32),
+        vm((R, R), BF16), vm((R, R), BF16), vm((R, COLS), BF16),
         dma((2, NZ)), dma, dma((NZ,)), dma((NZ,)), dma((2, 4, 2, 2)), dma((2, 4, 2, 2)),
-        dma((2, 4, 2, 2)), dma((2, 4, 2, 2)), dma((2, 5, 2)), dma((2, 5, 2)),
-        dma((4,)), dma((4,)), dma((4,)), dma((4,)), dma, dma,
+        dma((2, 4, 2, 2)), dma((2, 4, 2, 2)), dma((5,)), dma((5,)),
+        dma((5,)), dma((5,)), dma((4,)), dma((4,)), dma, dma,
     ]
     whole, hbm = pl.BlockSpec(memory_space=pltpu.VMEM), pl.BlockSpec(memory_space=pl.ANY)
     return pl.pallas_call(
@@ -429,12 +443,13 @@
         name="gather",
         out_shape=(
             pltpu.VMEM((NZ, PAIR, COLS), F32),
-            pltpu.VMEM((NZ, PAIR, R), F32),
+            pltpu.VMEM((NZ, PAIR, R), BF16),
+            pltpu.VMEM((NZ, PAIR, R), BF16),
             pltpu.VMEM((R, COLS), F32),
             pltpu.VMEM((8, R), F32),
         ),
         in_specs=[hbm, hbm, hbm],
-        out_specs=(whole, whole, whole, whole),
+        out_specs=(whole,) * 5,
         scratch_shapes=scratch,
         compiler_params=pltpu.CompilerParams(
             collective_id=0, has_side_effects=True, vmem_limit_bytes=40 << 20
@@ -443,31 +458,37 @@
 
 
 def result_kernel(
-    nm, u_ref, wt_ref, inv_ref, new_mom, new_factor, update, ub, fb, wh, wl, m_sem, u_sem, f_sem
+    nm, uh, ul, wt_ref, inv_ref, new_mom, new_factor, update, ub, fb, wh, wl, m_sem, u_sem, f_sem
 ):
+    steps = ROWS // TILE
+
     def tile(i):
         return pl.ds(i * TILE, TILE)
 
     copies = []
-    for i in range(ROWS // TILE):
-        copies.append(pltpu.make_async_copy(nm.at[tile(i)], new_mom.at[tile(i)], m_sem.at[i]))
+
+    def go(src, dst, sem):
+        copies.append(pltpu.make_async_copy(src, dst, sem))
         copies[-1].start()
-    inv = inv_ref[0:1, :]
-    wh[...], wl[...] = split(wt_ref[...])
-    for i in range(ROWS // TILE):
-        scaled = split(u_ref[tile(i), :] * (inv * (-step_size * math.sqrt(FF / R))))
-        ub[tile(i), :] = dot3(scaled, (wh[...], wl[...])).astype(BF16)
-        copies.append(pltpu.make_async_copy(ub.at[tile(i)], update.at[tile(i)], u_sem.at[i]))
-        copies[-1].start()
+
+    for i in range(0, steps, 2):
+        go(nm.at[tile(i)], new_mom.at[tile(i)], m_sem.at[i])
+    inv = jnp.swapaxes(inv_ref[...], 0, 1)[:, 0:1]
+    factor = wt_ref[...] * inv
+    wh[...], wl[...] = split(factor * (-step_size * math.sqrt(FF / R)))
+    for i in range(steps):
+        ub[tile(i), :] = dot3((uh[tile(i), :], ul[tile(i), :]), (wh[...], wl[...])).astype(BF16)
+        go(ub.at[tile(i)], update.at[tile(i)], u_sem.at[i])
+        if i < steps // 2:
+            go(nm.at[tile(2 * i + 1)], new_mom.at[tile(2 * i + 1)], m_sem.at[2 * i + 1])
         if i == 0:
-            fb[...] = jnp.swapaxes(wt_ref[...], 0, 1) * inv
-            copies.append(pltpu.make_async_copy(fb, new_factor, f_sem))
-            copies[-1].start()
+            fb[...] = jnp.swapaxes(wt_ref[...] * inv, 0, 1)
+            go(fb, new_factor, f_sem)
     for copy in copies:
         copy.wait()
 
 
-def results(nm, u, wt, inv):
+def results(nm, uh, ul, wt, inv):
     vmem, hbm = pl.BlockSpec(memory_space=pltpu.VMEM), pl.BlockSpec(memory_space=pl.ANY)
     dma = pltpu.SemaphoreType.DMA
     return pl.pallas_call(
@@ -478,7 +499,7 @@
             jax.ShapeDtypeStruct((COLS, R), F32),
             jax.ShapeDtypeStruct((ROWS, COLS), BF16),
         ),
-        in_specs=[vmem, vmem, vmem, vmem],
+        in_specs=[vmem] * 5,
         out_specs=(hbm, hbm, hbm),
         scratch_shapes=[
             pltpu.VMEM((ROWS, COLS), BF16),
@@ -490,12 +511,12 @@
             dma,
         ],
         compiler_params=pltpu.CompilerParams(vmem_limit_bytes=32 << 20),
-    )(nm, u, wt, inv)
+    )(nm, uh, ul, wt, inv)
 
 
 def local(momentum, gradient, right_factor):
-    nm, u, wt, inv = gather(momentum, gradient, right_factor)
-    return results(nm.reshape(ROWS, COLS), u.reshape(ROWS, R), wt, inv)
+    nm, uh, ul, wt, inv = gather(momentum, gradient, right_factor)
+    return results(nm.reshape(ROWS, COLS), uh.reshape(ROWS, R), ul.reshape(ROWS, R), wt, inv)
 
 
 def solution(mesh):

time: 74.2 us -> 71.8 us (0.968)
  Pallas kernels: 73.4 us -> 70.9 us
    pallas_call x1, Pallas kernels: 69.7 us -> 67.1 us  [gather(): pl.pallas_call(gather_kernel, name='gather', out_shape=(pltpu.VMEM((NZ, P...]
where the time goes in v1:
time: 71.8 us; the launch traced here: 71.7 us
  Pallas kernels  70.9 us (99%)
  between operations  0.8 us (1%)
    pallas_call x1, Pallas kernels, gather(): pl.pallas_call(gather_kernel, name='gather', out_shape=(pltpu.VMEM((NZ, P...  67.1 us
    pallas_call x1, Pallas kernels, results(): pl.pallas_call(result_kernel, name='results', out_shape=(jax.ShapeDtypeSt...  3.86 us

profile of v1, /device:TPU:1, one launch (start us, length us, event | category | flops | bytes accessed | tf_op | source)
XLA Modules:
  0.0 71.7 jit_solution(9162786850451290593)
XLA Ops:
  0.6 67.1 %gather.1 = (f32[8,224,512]{2,1,0:T(8,128)S(1)}, bf16[8,224,256]{2,1,0:T(8,128)(2,1)S(1)}, bf16[8,224,256]{2,1,0:T(8,128)(2,1)S(1)}, f32[256,512]{1,0:T(8,128)S(1)}, f32[8,256]{1,0:T(8,128)S(1)}) custom-call(f32[1792,512]{1,0:T(8,128)} %mom.1, bf16[1792,512]{1,0:T(8,128)(2,1)} %grad.1, f32[512,256]{1,0:T(8,128)} %q_hbm.1), custom_call_target="tpu_custom_call" | custom-call | tf_op jit(solution)/shard_map/gather/pallas_call | solution.py:441
  67.7 3.9 %results.1 = (f32[1792,512]{1,0:T(8,128)}, f32[512,256]{1,0:T(8,128)}, bf16[1792,512]{1,0:T(8,128)(2,1)}) custom-call(f32[1792,512]{1,0:T(8,128)S(1)} %bitcast.3, bf16[1792,256]{1,0:T(8,128)(2,1)S(1)} %bitcast.4, bf16[1792,256]{1,0:T(8,128)(2,1)S(1)} %bitcast.5, f32[256,512]{1,0:T(8,128)S(1)} %get-tuple-element.11.wt_ref, f32[8,256]{1,0:T(8,128)S(1)} %get-tuple-element.12.inv_ref), custom_call_target="tpu_custom_call" | custom-call | tf_op jit(solution)/shard_map/results/pallas_call | solution.py:494

commit v2 on v1

--- a/solution.py
+++ b/solution.py
@@ -391,9 +391,9 @@
     wt_out[...] = wt
     square = wt * wt
     square = (square[:, :128] + square[:, 128:256]) + (square[:, 256:384] + square[:, 384:])
-    cs[...] = jnp.broadcast_to(jnp.sum(jnp.swapaxes(square, 0, 1), axis=0, keepdims=True), (8, R))
+    cs[...] = jnp.sum(jnp.swapaxes(square, 0, 1), axis=0, keepdims=True)
     to_all(lambda peer: cs, csr, n_s, n_r, "rep")
-    csr[pl.ds(r, 1)] = cs[...].reshape(1, 8, R)
+    csr[pl.ds(r, 1)] = cs[...].reshape(1, 1, R)
 
     lth[...], ltl[...] = split(jnp.swapaxes(M[...], 0, 1))
     wh[...] = wt.astype(BF16)
@@ -409,7 +409,7 @@
         nm_out[zs] = momb[k] - keep_share * dot(u[0], wh[...])
 
     span_wait(csr, n_r)
-    inv_out[...] = 1.0 / jnp.sqrt(total(csr) / D + norm_eps)
+    inv_out[...] = jnp.broadcast_to(1.0 / jnp.sqrt(total(csr) / D + norm_eps), (8, R))
     for copy in sends:
         copy.wait_send()
     for k, ref in enumerate((g1, g2, gf.at[0])):
@@ -431,7 +431,7 @@
         vm((2, 8, R), F32),
         vm((R, R), F32),
         vm((2, 128, COLS), F32), vm((2, 16, 8, COLS), F32), vm((2, 16, 8, COLS), F32), vm((2, 8, COLS), F32),
-        vm((16, R), F32), vm((8, R), F32), vm((16, 8, R), F32),
+        vm((16, R), F32), vm((1, R), F32), vm((16, 1, R), F32),
         vm((R, R), BF16), vm((R, R), BF16), vm((R, COLS), BF16),
         dma((2, NZ)), dma, dma((NZ,)), dma((NZ,)), dma((2, 4, 2, 2)), dma((2, 4, 2, 2)),
         dma((2, 4, 2, 2)), dma((2, 4, 2, 2)), dma((5,)), dma((5,)),

time: 71.8 us -> 71.1 us (level)
  no operation moved by 1% of the time
where the time goes in v2:
time: 71.1 us; the launch traced here: 71 us
  Pallas kernels  70.2 us (99%)
  between operations  0.8 us (1%)
    pallas_call x1, Pallas kernels, gather(): pl.pallas_call(gather_kernel, name='gather', out_shape=(pltpu.VMEM((NZ, P...  66.4 us
    pallas_call x1, Pallas kernels, results(): pl.pallas_call(result_kernel, name='results', out_shape=(jax.ShapeDtypeSt...  3.86 us

profile of v2, /device:TPU:1, one launch (start us, length us, event | category | flops | bytes accessed | tf_op | source)
XLA Modules:
  0.0 71.0 jit_solution(4269605775547919396)
XLA Ops:
  0.6 66.4 %gather.1 = (f32[8,224,512]{2,1,0:T(8,128)S(1)}, bf16[8,224,256]{2,1,0:T(8,128)(2,1)S(1)}, bf16[8,224,256]{2,1,0:T(8,128)(2,1)S(1)}, f32[256,512]{1,0:T(8,128)S(1)}, f32[8,256]{1,0:T(8,128)S(1)}) custom-call(f32[1792,512]{1,0:T(8,128)} %mom.1, bf16[1792,512]{1,0:T(8,128)(2,1)} %grad.1, f32[512,256]{1,0:T(8,128)} %q_hbm.1), custom_call_target="tpu_custom_call" | custom-call | tf_op jit(solution)/shard_map/gather/pallas_call | solution.py:441
  67.0 3.9 %results.1 = (f32[1792,512]{1,0:T(8,128)}, f32[512,256]{1,0:T(8,128)}, bf16[1792,512]{1,0:T(8,128)(2,1)}) custom-call(f32[1792,512]{1,0:T(8,128)S(1)} %bitcast.3, bf16[1792,256]{1,0:T(8,128)(2,1)S(1)} %bitcast.4, bf16[1792,256]{1,0:T(8,128)(2,1)S(1)} %bitcast.5, f32[256,512]{1,0:T(8,128)S(1)} %get-tuple-element.11.wt_ref, f32[8,256]{1,0:T(8,128)S(1)} %get-tuple-element.12.inv_ref), custom_call_target="tpu_custom_call" | custom-call | tf_op jit(solution)/shard_map/results/pallas_call | solution.py:494
